TPU v7x, 32 devices: a whole 2x2x4 slice. The times are simulated.
32 devices in a mesh: dp: 4 (over z), expert: 8 (over y, x, core).
Axes of the slice: x: 2, y: 2, z: 4, core: 2. Of those that a mesh axis runs over, the one named last changes fastest.
Arguments:
- tokens: bfloat16 [4096, 4096], P(('dp', 'expert')), may hold values from -6 to 6
- cotangent: bfloat16 [4096, 4096], P(('dp', 'expert')), may hold values from -0.796875 to 0.796875
- router_probs: float32 [4096, 4], P(('dp', 'expert')), may hold values from 0.1 to 1
- routing: int32 [4096, 4], P(('dp', 'expert')), may hold values from 0 to 31, all different within a row
- hot_marks: int32 [32], replicated, may hold values from 0 to 1, as said below
- cap_counts: int32 [32], replicated, may hold values from 8 to 16, as said below
- gate_up: bfloat16 [32, 2, 4096, 768], P(('dp', 'expert')), may hold values from -0.09375 to 0.09375
- adapter_in: bfloat16 [32, 32, 768], P(('dp', 'expert')), may hold values from -0.21875 to 0.21875
- adapter_out: bfloat16 [32, 32, 4096], P(('dp', 'expert')), may hold values from -0.09375 to 0.09375
Outputs:
- in_gradient: float32 [32, 32, 768], P(('dp', 'expert'))
- out_gradient: float32 [32, 32, 4096], P(('dp', 'expert'))
Inputs may be any that keep to these rules, and one draw needn't show every extreme that they name: `routing`: each token names 4 different experts. `hot_marks`: of every two experts whose numbers differ only in the bit of value 8 / 2, exactly one is marked. `cap_counts`: some expert's count equals 16.
All inputs are finite; a program needn't handle non-finite values.
Results may differ from a plain program's by a relative error of at most 0.005.
Values may be sent and summed in bfloat16 or wider, within the bound.
A program may use at most 192 MiB of HBM per device.

v0:
```python
import jax
import jax.numpy as jnp
from jax import lax
from jax.sharding import PartitionSpec as P

adapter_scale_factor = 2.0


def hidden_units(inputs, weights):
    gate_out = jnp.dot(inputs, weights[0], preferred_element_type=jnp.float32)
    up_out = jnp.dot(inputs, weights[1], preferred_element_type=jnp.float32)
    return (jax.nn.silu(gate_out) * up_out).astype(jnp.bfloat16)


def adapter_grads(hidden_state_rows, scaled_adapter_output, adapter_down_matrix, adapter_up_matrix):
    rank_projected_rows = (
        adapter_scale_factor
        * jnp.einsum(
            "pn,cn->pc", hidden_state_rows, adapter_down_matrix, preferred_element_type=jnp.float32
        )
    ).astype(jnp.bfloat16)
    rank_gradient_rows = (
        adapter_scale_factor
        * jnp.einsum(
            "vw,cw->vc",
            scaled_adapter_output,
            adapter_up_matrix,
            preferred_element_type=jnp.float32,
        )
    ).astype(jnp.bfloat16)
    grad_first = jnp.einsum(
        "mr,mf->rf", rank_gradient_rows, hidden_state_rows, preferred_element_type=jnp.float32
    )
    grad_second = jnp.einsum(
        "mr,md->rd", rank_projected_rows, scaled_adapter_output, preferred_element_type=jnp.float32
    )
    return (grad_first, grad_second)


def body(
    tokens,
    cotangent,
    router_probs,
    routing,
    hot_marks,
    cap_counts,
    gate_up,
    adapter_in,
    adapter_out,
):
    tok_count, model_width = tokens.shape
    top_count = routing.shape[1]
    expert_total = cap_counts.shape[0]
    capacity = tok_count * top_count // expert_total
    pair_count = tok_count * top_count
    flat_route = routing.reshape(pair_count)
    expert_ids = jnp.arange(expert_total, dtype=jnp.int32)
    onehot = (flat_route[:, None] == expert_ids[None, :]).astype(jnp.int32)
    order_rank = jnp.sum((jnp.cumsum(onehot, axis=0) - onehot) * onehot, axis=1)
    own_cap = jnp.sum(onehot * cap_counts[None, :], axis=1)
    is_marked = jnp.sum(onehot * hot_marks[None, :], axis=1)
    first_block = order_rank < own_cap
    second_block = (is_marked == 1) & (order_rank >= own_cap) & (order_rank < own_cap + capacity)
    offset = order_rank - own_cap
    per_dest = 2 * capacity
    extra_pos = capacity + offset
    slot_total = expert_total * per_dest
    slot_index = jnp.where(
        first_block,
        order_rank * expert_total + flat_route,
        jnp.where(second_block, extra_pos * expert_total + flat_route, slot_total),
    )
    pair_ids = jnp.arange(pair_count, dtype=jnp.int32)
    slot_source = (
        jnp.full((slot_total + 1,), -1, jnp.int32).at[slot_index].set(pair_ids)[:slot_total]
    )
    valid_slots = slot_source >= 0
    safe_ids = jnp.maximum(slot_source, 0)
    token_ids = safe_ids // top_count
    factor = jnp.where(valid_slots, router_probs.reshape(pair_count)[safe_ids], 0.0)
    token_rows = jnp.where(valid_slots[:, None], tokens[token_ids], jnp.zeros((), jnp.bfloat16))
    scaled_rows = (factor[:, None] * cotangent[token_ids].astype(jnp.float32)).astype(jnp.bfloat16)
    shaped_rows = token_rows.reshape(per_dest, expert_total, model_width)
    shaped_scaled = scaled_rows.reshape(per_dest, expert_total, model_width)
    arrived_rows, arrived_scaled = (
        lax.all_to_all(shaped_rows, ("dp", "expert"), split_axis=1, concat_axis=1, tiled=True),
        lax.all_to_all(shaped_scaled, ("dp", "expert"), split_axis=1, concat_axis=1, tiled=True),
    )
    first_inputs = arrived_rows[:capacity].reshape(capacity * expert_total, model_width)
    first_scaled = arrived_scaled[:capacity].reshape(capacity * expert_total, model_width)
    extra_inputs = arrived_rows[capacity:].reshape(
        (per_dest - capacity) * expert_total, model_width
    )
    extra_scaled = arrived_scaled[capacity:].reshape(
        (per_dest - capacity) * expert_total, model_width
    )
    own_weights = gate_up[0]
    own_first = adapter_in[0]
    own_second = adapter_out[0]
    own_hidden = hidden_units(first_inputs, own_weights)
    grad_first, grad_second = adapter_grads(own_hidden, first_scaled, own_first, own_second)
    extra_hidden = hidden_units(extra_inputs, own_weights)
    extra_first, extra_second = adapter_grads(extra_hidden, extra_scaled, own_first, own_second)
    grad_first = grad_first + extra_first
    grad_second = grad_second + extra_second
    return (grad_first[None], grad_second[None])


def solution(mesh):
    in_specs = (
        P(("dp", "expert"), None),
        P(("dp", "expert"), None),
        P(("dp", "expert"), None),
        P(("dp", "expert"), None),
        P(),
        P(),
        P(("dp", "expert"), None, None, None),
        P(("dp", "expert"), None, None),
        P(("dp", "expert"), None, None),
    )
    out_specs = (P(("dp", "expert"), None, None), P(("dp", "expert"), None, None))
    return jax.shard_map(body, mesh=mesh, in_specs=in_specs, out_specs=out_specs, check_vma=False)
```

profile of v0, /device:TPU:0, one launch (start us, length us, event | category | flops | bytes accessed | tf_op | source)
XLA Modules:
  0.0 478.2 jit_solution(10360248524393517413)
XLA Ops:
  0.6 0.9 copy.23
  1.7 0.1 reshape.150
  1.9 1.2 reduce-window.6
  3.0 0.2 slice_reduce_fusion
  3.3 0.8 select_reduce_fusion
  4.1 2.5 scatter_custom_fusion
  6.6 0.8 copy.27
  7.5 6.9 %gather_fusion = f32[1024]{0:T(1024)S(1)} fusion(f32[512]{0:T(512)S(1)} %reshape.151, s32[1024]{0:T(1024)S(1)} %get-tuple-element.9), kind=kCustom, calls=%fused_computation | custom fusion | bytes 12288 | tf_op jit(solution)/shard_map/gather | solution.py:80
  14.6 7.7 %gather_fusion.1 = bf16[1024,4096]{1,0:T(8,128)(2,1)} fusion(bf16[128,4096]{1,0:T(8,128)(2,1)S(1)} %copy-done, s32[1024]{0:T(1024)S(1)} %get-tuple-element.10), kind=kCustom, calls=%fused_computation.1 | custom fusion | bytes 16781312 | tf_op jit(solution)/shard_map/gather | solution.py:82
  22.4 11.4 %convert.1 = f32[32,32,4096]{2,1,0:T(8,128)} convert(bf16[32,32,4096]{2,1,0:T(8,128)(2,1)} %bitcast.78) | non-fusion elementwise | flops 4194304 | bytes 25165824 | tf_op jit(solution)/shard_map/convert_element_type | solution.py:82
  33.8 16.9 %fusion = bf16[32,32,4096]{2,0,1:T(8,128)(2,1)} fusion(f32[32,32,4096]{2,1,0:T(8,128)} %convert.1, f32[32,32]{0,1:T(8,128)S(1)} %copy.28), kind=kLoop, calls=%fused_computation.5 | loop fusion | flops 8388608 | bytes 25169920 | tf_op jit(solution)/shard_map/convert_element_type | solution.py:82
  50.6 7.6 %all-to-all-start = ((bf16[32,32,4096]{2,0,1:T(8,128)(2,1)}), bf16[32,32,4096]{2,0,1:T(8,128)(2,1)}, u32[]{:S(2)}, u32[]{:S(2)}) async-start(bf16[32,32,4096]{2,0,1:T(8,128)(2,1)} %fusion), calls=%async_computation | async-start | bytes 16777216 | tf_op jit(solution)/shard_map/all_to_all | solution.py:87
  58.3 7.8 %gather_fusion.2 = bf16[1024,4096]{1,0:T(8,128)(2,1)} fusion(bf16[128,4096]{1,0:T(8,128)(2,1)S(1)} %copy-done.2, s32[1024]{0:T(1024)S(1)} %get-tuple-element.10), kind=kCustom, calls=%fused_computation.2 | custom fusion | bytes 16781312 | tf_op jit(solution)/shard_map/gather | solution.py:81
  66.1 16.3 %copy_select_fusion = bf16[32,32,4096]{2,0,1:T(8,128)(2,1)} fusion(bf16[32,32,4096]{2,1,0:T(8,128)(2,1)} %bitcast.77, pred[32,32]{0,1:T(8,128)(4,1)S(1)} %copy.31), kind=kLoop, calls=%fused_computation.6 | loop fusion | flops 4194304 | bytes 16778240 | tf_op jit(solution)/shard_map/jit(_where)/select_n | solution.py:81
  82.5 161.8 %all-to-all-done = bf16[32,32,4096]{2,0,1:T(8,128)(2,1)} async-done(((bf16[32,32,4096]{2,0,1:T(8,128)(2,1)}), bf16[32,32,4096]{2,0,1:T(8,128)(2,1)}, u32[]{:S(2)}, u32[]{:S(2)}) %all-to-all-start) | async-done | bytes 8388640 | tf_op jit(solution)/shard_map/all_to_all | solution.py:87
  244.3 3.7 all-to-all-start.1
  248.0 5.2 %fusion.50 = (bf16[16,32,4096]{2,0,1:T(8,128)(2,1)}, bf16[16,32,4096]{2,0,1:T(8,128)(2,1)S(1)}) fusion(bf16[32,32,4096]{2,0,1:T(8,128)(2,1)} %all-to-all-done), kind=kLoop, calls=%fused_computation.74 | loop fusion | bytes 16777216 | tf_op jit(solution)/shard_map/slice | solution.py:94
  253.2 4.2 copy.36
  257.4 176.7 %all-to-all-done.1 = bf16[32,32,4096]{2,0,1:T(8,128)(2,1)} async-done(((bf16[32,32,4096]{2,0,1:T(8,128)(2,1)}), bf16[32,32,4096]{2,0,1:T(8,128)(2,1)}, u32[]{:S(2)}, u32[]{:S(2)}) %all-to-all-start.1) | async-done | bytes 8388640 | tf_op jit(solution)/shard_map/all_to_all | solution.py:86
  434.1 4.3 fusion.51
  438.5 2.3 copy.37
  440.8 0.6 slice-done.2
  441.5 3.5 fusion.7
  444.9 3.5 multiply_convert_fusion.1
  448.5 2.3 copy.39
  450.8 3.6 fusion.5
  454.5 3.5 multiply_convert_fusion
  458.0 4.3 copy.38
  462.3 3.4 fusion.24
  465.7 3.8 fusion.23
  469.4 4.2 fusion.13
  473.6 4.4 fusion.18
  (34 shorter events, 0.8 us)
Async XLA Ops:
  0.6 14.0 %copy-start = (bf16[128,4096]{1,0:T(8,128)(2,1)S(1)}, bf16[128,4096]{1,0:T(8,128)(2,1)}, u32[]{:S(2)}) copy-start(bf16[128,4096]{1,0:T(8,128)(2,1)} %param.10) | copy-start | bytes 3145732
  50.6 7.7 %copy-start.2 = (bf16[128,4096]{1,0:T(8,128)(2,1)S(1)}, bf16[128,4096]{1,0:T(8,128)(2,1)}, u32[]{:S(2)}) copy-start(bf16[128,4096]{1,0:T(8,128)(2,1)} %param.9) | copy-start | bytes 3145732
  50.6 193.7 %all-to-all-start = ((bf16[32,32,4096]{2,0,1:T(8,128)(2,1)}), bf16[32,32,4096]{2,0,1:T(8,128)(2,1)}, u32[]{:S(2)}, u32[]{:S(2)}) async-start(bf16[32,32,4096]{2,0,1:T(8,128)(2,1)} %fusion), calls=%async_computation | async-start | bytes 16777216 | tf_op jit(solution)/shard_map/all_to_all | solution.py:87
  244.3 189.8 %all-to-all-start.1 = ((bf16[32,32,4096]{2,0,1:T(8,128)(2,1)}), bf16[32,32,4096]{2,0,1:T(8,128)(2,1)}, u32[]{:S(2)}, u32[]{:S(2)}) async-start(bf16[32,32,4096]{2,0,1:T(8,128)(2,1)} %copy_select_fusion), calls=%async_computation.1 | async-start | bytes 16777216 | tf_op jit(solution)/shard_map/all_to_all | solution.py:86
  434.1 6.7 %slice-start = ((s8[12582912]{0:T(1024)(128)(4,1)}), s8[4194304]{0:T(1024)(128)(4,1)S(1)}, s32[]{:S(2)}) async-start(s8[12582912]{0:T(1024)(128)(4,1)} %bitcast.86), calls=%async_computation.2 | async-start | bytes 8388608
  434.1 6.7 %slice-start.1 = ((s8[12582912]{0:T(1024)(128)(4,1)}), s8[4194304]{0:T(1024)(128)(4,1)S(1)}, s32[]{:S(2)}) async-start(s8[12582912]{0:T(1024)(128)(4,1)} %bitcast.86), calls=%async_computation.3 | async-start | bytes 8388608
  438.5 3.0 slice-start.2
  454.4 3.6 copy-start.3
  458.0 4.3 copy-start.5
  462.3 3.4 copy-start.4
  469.4 8.6 %copy-start.1 = (bf16[128,4096]{1,0:T(8,128)(2,1)S(1)}, bf16[128,4096]{1,0:T(8,128)(2,1)}, u32[]{:S(2)}) copy-start(bf16[128,4096]{1,0:T(8,128)(2,1)} %param.10) | copy-start | bytes 3145732
where the time goes:
time: 485 us; the launch traced here: 478 us
  waiting for transfers between devices  339 us (70%)
  local copies, waits for them, and re-layouts  50.8 us (10%)
  other arithmetic  46.6 us (10%)
  matrix products  29.9 us (6%)
  starting transfers between devices  11.3 us (2%)
    all_to_all x1, waiting for transfers between devices, body(): lax.all_to_all(shaped_rows, ('dp', 'expert'), split_axis=1, concat_axis=1...  177 us
    all_to_all x1, waiting for transfers between devices, body(): lax.all_to_all(shaped_scaled, ('dp', 'expert'), split_axis=1, concat_axis...  162 us
    convert_element_type x1, other arithmetic, body(): (factor[:, None] * cotangent[token_ids].astype(jnp.float32)).astype(jnp.b...  16.9 us
    select_n x1, other arithmetic, body(): jnp.where(valid_slots[:, None], tokens[token_ids], jnp.zeros((), jnp.bflo...  16.3 us
    unnamed x24, local copies, waits for them, and re-layouts  15.5 us
    convert_element_type x1, other arithmetic, body(): cotangent[token_ids].astype(jnp.float32)  11.4 us
  transfers between devices with their start and end apart: 2, of which 2 were waited for; matrix products, arithmetic and copies ran while one was open for 7% of the time, Pallas kernels for 0%

commit v1 on v0

v1 whole, which is shorter than its diff:
```python
import jax
import jax.numpy as jnp
from jax import lax
from jax.sharding import PartitionSpec as P

adapter_scale_factor = 2.0


def hidden_units(inputs, weights):
    gate_out = jnp.dot(inputs, weights[0], preferred_element_type=jnp.float32)
    up_out = jnp.dot(inputs, weights[1], preferred_element_type=jnp.float32)
    return (jax.nn.silu(gate_out) * up_out).astype(jnp.bfloat16)


def body(
    tokens,
    cotangent,
    router_probs,
    routing,
    hot_marks,
    cap_counts,
    gate_up,
    adapter_in,
    adapter_out,
):
    tok_count, model_width = tokens.shape
    top_count = routing.shape[1]
    expert_total = cap_counts.shape[0]
    capacity = tok_count * top_count // expert_total
    per_dest = 2 * capacity
    dp_count = lax.axis_size("dp")
    group = lax.axis_size("expert")

    routed = jnp.concatenate([routing.astype(jnp.float32), router_probs], axis=1)
    routed = lax.all_gather(routed, "dp", axis=0, tiled=False)
    all_tokens = lax.all_gather(tokens, "dp", axis=0, tiled=False)
    all_cotangent = lax.all_gather(cotangent, "dp", axis=0, tiled=False)

    first_expert = lax.axis_index("dp") * group
    own_experts = first_expert + jnp.arange(group, dtype=jnp.int32)
    limits = cap_counts + capacity * hot_marks
    own_limits = lax.dynamic_slice_in_dim(limits, first_expert, group).astype(jnp.float32)
    routes = routed[:, :, :top_count]
    probs = routed[:, :, top_count:]
    named = routes[:, None, :, :] == own_experts.astype(jnp.float32)[None, :, None, None]
    member = jnp.any(named, axis=3)
    weight = jnp.sum(jnp.where(named, probs[:, None, :, :], 0.0), axis=3)
    at = jnp.arange(tok_count, dtype=jnp.int32)
    earlier = (at[:, None] < at[None, :]).astype(jnp.bfloat16)
    rank = jnp.einsum(
        "bet,tu->beu", member.astype(jnp.bfloat16), earlier, preferred_element_type=jnp.float32
    )
    kept = member & (rank < own_limits[None, :, None])
    column = jnp.where(kept, rank, -1.0).astype(jnp.int32)
    slots = jnp.arange(per_dest, dtype=jnp.int32)
    chosen = column[:, :, None, :] == slots[None, None, :, None]
    factor = jnp.sum(jnp.where(chosen, weight[:, :, None, :], 0.0), axis=3)
    chosen = chosen.astype(jnp.bfloat16).reshape(dp_count, group * per_dest, tok_count)
    factor = factor.reshape(dp_count, group * per_dest)

    def exchange(rows):
        rows = rows.reshape(dp_count, group, per_dest, model_width).swapaxes(0, 1)
        rows = lax.all_to_all(rows, "expert", split_axis=0, concat_axis=0, tiled=True)
        return rows.reshape(dp_count * group * per_dest, model_width)

    token_rows = jnp.einsum(
        "bst,btd->bsd", chosen, all_tokens, preferred_element_type=jnp.float32
    ).astype(jnp.bfloat16)
    inputs = exchange(token_rows)
    cotangent_rows = jnp.einsum(
        "bst,btd->bsd", chosen, all_cotangent, preferred_element_type=jnp.float32
    )
    scaled = exchange((factor[:, :, None] * cotangent_rows).astype(jnp.bfloat16))

    hidden = hidden_units(inputs, gate_up[0])
    low = (
        adapter_scale_factor
        * jnp.einsum("pn,cn->pc", hidden, adapter_in[0], preferred_element_type=jnp.float32)
    ).astype(jnp.bfloat16)
    back = (
        adapter_scale_factor
        * jnp.einsum("vw,cw->vc", scaled, adapter_out[0], preferred_element_type=jnp.float32)
    ).astype(jnp.bfloat16)
    grad_first = jnp.einsum("mr,mf->rf", back, hidden, preferred_element_type=jnp.float32)
    grad_second = jnp.einsum("mr,md->rd", low, scaled, preferred_element_type=jnp.float32)
    return (grad_first[None], grad_second[None])


def solution(mesh):
    in_specs = (
        P(("dp", "expert"), None),
        P(("dp", "expert"), None),
        P(("dp", "expert"), None),
        P(("dp", "expert"), None),
        P(),
        P(),
        P(("dp", "expert"), None, None, None),
        P(("dp", "expert"), None, None),
        P(("dp", "expert"), None, None),
    )
    out_specs = (P(("dp", "expert"), None, None), P(("dp", "expert"), None, None))
    return jax.shard_map(body, mesh=mesh, in_specs=in_specs, out_specs=out_specs, check_vma=False)
```

time: 485 us -> 330 us (0.68); the launches traced: 478 us -> 329 us
  waiting for transfers between devices: 339 us -> 222 us
  other arithmetic: 46.6 us -> 2.71 us
  local copies, waits for them, and re-layouts: 50.8 us -> 15.6 us
  matrix products: 29.9 us -> 49.7 us
  blocking collectives: 0 us -> 14.8 us
  between operations: 1.04 us -> 14.1 us
    all_to_all x2, waiting for transfers between devices: 339 us -> 71.7 us  [exchange(): lax.all_to_all(rows, 'expert', split_axis=0, concat_axis=0, tiled=True)]
    all_gather x0 -> x2, waiting for transfers between devices: none -> 149 us  [the longest x1 81 us: body(): all_cotangent = lax.all_gather(cotangent, 'dp', axis=0, tiled=False)]
    convert_element_type x3, other arithmetic: 28.3 us -> 0.77 us  [the longest x1 0.68 us: body(): routing.astype(jnp.float32)]
    gather x4 -> x0, local copies, waits for them, and re-layouts: 22.5 us -> none  [the longest x1 7.8 us: body(): tokens[token_ids]]
    select_n x3 -> x0, other arithmetic: 16.4 us -> none  [the longest x1 16.3 us: body(): jnp.where(valid_slots[:, None], tokens[token_ids], jnp.zeros((), jnp.bflo...]
    unnamed x24 -> x4, local copies, waits for them, and re-layouts: 15.5 us -> 0.02 us
    reshape x2, local copies, waits for them, and re-layouts: 0.21 us -> 15.4 us  [exchange(): rows = rows.reshape(dp_count, group, per_dest, model_width).swapaxes(0, 1)]
    all_gather x0 -> x1, blocking collectives: none -> 14.8 us  [body(): routed = lax.all_gather(routed, 'dp', axis=0, tiled=False)]
  transfers between devices with their start and end apart: 2 -> 4, of which waited for: 2 -> 3; matrix products, arithmetic and copies ran while one was open for 7% -> 12% of each run, Pallas kernels for 0% -> 0%
where the time goes in v1:
time: 330 us; the launch traced here: 329 us
  waiting for transfers between devices  222 us (67%)
  matrix products  49.7 us (15%)
  local copies, waits for them, and re-layouts  15.6 us (5%)
  blocking collectives  14.8 us (4%)
  between operations  14.1 us (4%)
  starting transfers between devices  10.2 us (3%)
    all_gather x1, waiting for transfers between devices, body(): all_cotangent = lax.all_gather(cotangent, 'dp', axis=0, tiled=False)  81 us
    all_to_all x2, waiting for transfers between devices, exchange(): lax.all_to_all(rows, 'expert', split_axis=0, concat_axis=0, tiled=True)  71.7 us
    all_gather x1, waiting for transfers between devices, body(): all_tokens = lax.all_gather(tokens, 'dp', axis=0, tiled=False)  67.8 us
    reshape x2, local copies, waits for them, and re-layouts, exchange(): rows = rows.reshape(dp_count, group, per_dest, model_width).swapaxes(0, 1)  15.4 us
    all_gather x1, blocking collectives, body(): routed = lax.all_gather(routed, 'dp', axis=0, tiled=False)  14.8 us
    dot_general x1, matrix products, hidden_units(): gate_out = jnp.dot(inputs, weights[0], preferred_element_type=jnp.float32)  11.2 us
    dot_general x1, matrix products, hidden_units(): up_out = jnp.dot(inputs, weights[1], preferred_element_type=jnp.float32)  10.9 us
    all_to_all x2, starting transfers between devices, exchange(): lax.all_to_all(rows, 'expert', split_axis=0, concat_axis=0, tiled=True)  10.1 us
  transfers between devices with their start and end apart: 4, of which 3 were waited for; matrix products, arithmetic and copies ran while one was open for 12% of the time, Pallas kernels for 0%

profile of v1, /device:TPU:0, one launch (start us, length us, event | category | flops | bytes accessed | tf_op | source)
XLA Modules:
  0.0 329.0 jit_solution(13913808964225844700)
XLA Ops:
  7.2 0.0 copy-start
  7.2 0.0 all-gather.8.cloned.1.call-start
  7.2 0.7 all-gather.8.cloned.1.call-update
  7.9 0.1 eq.45
  8.0 0.7 convert_element_type.34
  8.7 0.7 pad_maximum_fusion
  9.4 14.8 %all-gather = f32[512,8]{0,1:T(8,128)S(1)} all-gather(f32[128,8]{0,1:T(8,128)S(1)} %pad_maximum_fusion), channel_id=2, replica_groups=mesh['dp'=4,'expert'=8] {'dp'}, dimensions={0}, use_global_device_ids=true | all-gather | bytes 20480 | tf_op jit(solution)/shard_map/all_gather | solution.py:35
  24.2 0.7 multiply_add_fusion
  24.9 0.1 dynamic-slice_convert_fusion
  24.9 0.1 compare_reduce_fusion
  25.0 0.1 select_convert_fusion
  25.1 0.2 bitcast_compare_fusion
  25.3 67.8 %all-gather.8.cloned.1.call-done = bf16[512,4096]{1,0:T(8,128)(2,1)} async-done(((bf16[128,4096]{1,0:T(8,128)(2,1)}), bf16[512,4096]{1,0:T(8,128)(2,1)}) %all-gather.8.cloned.1.call-update) | async-done | bytes 4194320 | tf_op jit(solution)/shard_map/all_gather | solution.py:36
  93.1 7.7 %convolution_convert_fusion = bf16[4,256,4096]{2,1,0:T(8,128)(2,1)} fusion(pred[4,256,128]{2,1,0:T(32,128)(4,1)S(1)} %bitcast_compare_fusion, bf16[4,128,4096]{2,1,0:T(8,128)(2,1)} %bitcast.55), kind=kOutput, calls=%fused_computation.3 | convolution fusion | flops 1077936128 | bytes 12713984 | tf_op jit(solution)/shard_map/bst,btd->bsd/dot_general | solution.py:66
  100.8 7.7 %copy.21 = bf16[4,8,32,4096]{3,2,0,1:T(8,128)(2,1)} copy(bf16[4,8,32,4096]{3,2,1,0:T(8,128)(2,1)} %bitcast.51) | data formatting | bytes 16777216 | tf_op jit(solution)/shard_map/reshape | solution.py:62
  108.5 4.9 %all-to-all-start.1 = ((bf16[8,4,32,4096]{3,2,1,0:T(8,128)(2,1)}), bf16[8,4,32,4096]{3,2,1,0:T(8,128)(2,1)}, u32[]{:S(2)}, u32[]{:S(2)}) async-start(bf16[8,4,32,4096]{3,2,1,0:T(8,128)(2,1)} %bitcast.53), calls=%async_computation.1 | async-start | bytes 16777216 | tf_op jit(solution)/shard_map/all_to_all | solution.py:63
  113.5 0.0 all-gather.6.cloned.1.call-start
  113.5 0.7 all-gather.6.cloned.1.call-update
  114.2 0.1 fusion.12
  114.3 0.2 select_reduce_fusion
  114.5 0.1 mul.35
  114.6 81.0 %all-gather.6.cloned.1.call-done = bf16[512,4096]{1,0:T(8,128)(2,1)} async-done(((bf16[128,4096]{1,0:T(8,128)(2,1)}), bf16[512,4096]{1,0:T(8,128)(2,1)}) %all-gather.6.cloned.1.call-update) | async-done | bytes 4194320 | tf_op jit(solution)/shard_map/all_gather | solution.py:37
  195.6 6.7 %multiply_convert_fusion = bf16[4,256,4096]{2,1,0:T(8,128)(2,1)} fusion(pred[4,256,128]{2,1,0:T(32,128)(4,1)S(1)} %bitcast_compare_fusion, bf16[4,128,4096]{2,1,0:T(8,128)(2,1)} %bitcast.56, f32[4,256]{1,0:T(4,128)S(1)} %mul.35), kind=kOutput, calls=%fused_computation | convolution fusion | flops 1082130432 | bytes 12718080 | tf_op jit(solution)/shard_map/bst,btd->bsd/dot_general | solution.py:70
  202.3 7.7 %copy.22 = bf16[4,8,32,4096]{3,2,0,1:T(8,128)(2,1)} copy(bf16[4,8,32,4096]{3,2,1,0:T(8,128)(2,1)} %bitcast.52) | data formatting | bytes 16777216 | tf_op jit(solution)/shard_map/reshape | solution.py:62
  210.0 0.0 all-to-all-done.1
  210.0 5.2 %all-to-all-start = ((bf16[8,4,32,4096]{3,2,1,0:T(8,128)(2,1)}), bf16[8,4,32,4096]{3,2,1,0:T(8,128)(2,1)}, u32[]{:S(2)}, u32[]{:S(2)}) async-start(bf16[8,4,32,4096]{3,2,1,0:T(8,128)(2,1)} %bitcast.54), calls=%async_computation | async-start | bytes 16777216 | tf_op jit(solution)/shard_map/all_to_all | solution.py:63
  215.2 10.9 %fusion = f32[1024,768]{1,0:T(8,128)S(1)} fusion(bf16[1024,4096]{1,0:T(8,128)(2,1)} %bitcast.11, bf16[1,2,4096,768]{3,2,1,0:T(8,128)(2,1)} %param.15), kind=kOutput, calls=%fused_computation.4 | convolution fusion | flops 6442450944 | bytes 17825792 | tf_op jit(solution)/shard_map/dot_general | solution.py:11
  226.1 11.2 %multiply_convert_fusion.1 = bf16[1024,768]{1,0:T(8,128)(2,1)S(1)} fusion(f32[1024,768]{1,0:T(8,128)S(1)} %fusion, bf16[1024,4096]{1,0:T(8,128)(2,1)} %bitcast.11, bf16[1,2,4096,768]{3,2,1,0:T(8,128)(2,1)} %param.15), kind=kOutput, calls=%fused_computation.11 | convolution fusion | flops 6447169536 | bytes 19398656 | tf_op jit(solution)/shard_map/dot_general | solution.py:10
  237.4 0.0 copy-start.1
  237.4 71.7 %all-to-all-done = bf16[8,4,32,4096]{3,2,1,0:T(8,128)(2,1)} async-done(((bf16[8,4,32,4096]{3,2,1,0:T(8,128)(2,1)}), bf16[8,4,32,4096]{3,2,1,0:T(8,128)(2,1)}, u32[]{:S(2)}, u32[]{:S(2)}) %all-to-all-start) | async-done | bytes 8388640 | tf_op jit(solution)/shard_map/all_to_all | solution.py:63
  309.1 6.9 %convolution_bitcast_fusion.1 = f32[1,32,768]{2,1,0:T(8,128)} fusion(bf16[1024,768]{1,0:T(8,128)(2,1)S(1)} %multiply_convert_fusion.1, bf16[1024,4096]{1,0:T(8,128)(2,1)} %bitcast.6, bf16[1,32,4096]{2,1,0:T(8,128)(2,1)S(1)} %copy-done), kind=kOutput, calls=%fused_computation.14 | convolution fusion | flops 318832640 | bytes 10321920 | tf_op jit(solution)/shard_map/mr,mf->rf/dot_general | solution.py:84
  316.0 6.2 %convolution_bitcast_fusion = f32[1,32,4096]{2,1,0:T(8,128)} fusion(bf16[1024,4096]{1,0:T(8,128)(2,1)} %bitcast.6, bf16[1024,768]{1,0:T(8,128)(2,1)S(1)} %multiply_convert_fusion.1, bf16[1,32,768]{2,1,0:T(8,128)(2,1)S(1)} %copy-done.1), kind=kOutput, calls=%fused_computation.10 | convolution fusion | flops 318832640 | bytes 10534912 | tf_op jit(solution)/shard_map/mr,md->rd/dot_general | solution.py:85
  (5 shorter events, 0.0 us)
Async XLA Ops:
  7.2 301.9 %copy-start = (bf16[1,32,4096]{2,1,0:T(8,128)(2,1)S(1)}, bf16[1,32,4096]{2,1,0:T(8,128)(2,1)}, u32[]{:S(2)}) copy-start(bf16[1,32,4096]{2,1,0:T(8,128)(2,1)} %param.17) | copy-start | bytes 786436
  7.2 85.9 %all-gather.8.cloned.1.call-start = ((), (), s32[]{:S(2)}) async-start(), calls=%async_computation.3 | async-start | bytes 5242880 | tf_op jit(solution)/shard_map/all_gather | solution.py:36
  108.5 101.5 %all-to-all-start.1 = ((bf16[8,4,32,4096]{3,2,1,0:T(8,128)(2,1)}), bf16[8,4,32,4096]{3,2,1,0:T(8,128)(2,1)}, u32[]{:S(2)}, u32[]{:S(2)}) async-start(bf16[8,4,32,4096]{3,2,1,0:T(8,128)(2,1)} %bitcast.53), calls=%async_computation.1 | async-start | bytes 16777216 | tf_op jit(solution)/shard_map/all_to_all | solution.py:63
  113.5 82.2 %all-gather.6.cloned.1.call-start = ((), (), s32[]{:S(2)}) async-start(), calls=%async_computation.2 | async-start | bytes 5242880 | tf_op jit(solution)/shard_map/all_gather | solution.py:37
  210.0 99.1 %all-to-all-start = ((bf16[8,4,32,4096]{3,2,1,0:T(8,128)(2,1)}), bf16[8,4,32,4096]{3,2,1,0:T(8,128)(2,1)}, u32[]{:S(2)}, u32[]{:S(2)}) async-start(bf16[8,4,32,4096]{3,2,1,0:T(8,128)(2,1)} %bitcast.54), calls=%async_computation | async-start | bytes 16777216 | tf_op jit(solution)/shard_map/all_to_all | solution.py:63
  237.4 78.6 %copy-start.1 = (bf16[1,32,768]{2,1,0:T(8,128)(2,1)S(1)}, bf16[1,32,768]{2,1,0:T(8,128)(2,1)}, u32[]{:S(2)}) copy-start(bf16[1,32,768]{2,1,0:T(8,128)(2,1)} %param.16) | copy-start | bytes 147460
Sparse Core Ops, SparseCore 0:
  9.6 83.4 all-gather.7
  115.9 79.7 all-gather.5

commit v2 on v1

--- a/solution.py
+++ b/solution.py
@@ -1,15 +1,47 @@
+import functools
+
 import jax
 import jax.numpy as jnp
 from jax import lax
+from jax.experimental import pallas as pl
+from jax.experimental.pallas import tpu as pltpu
 from jax.sharding import PartitionSpec as P
 
 adapter_scale_factor = 2.0
 
 
-def hidden_units(inputs, weights):
-    gate_out = jnp.dot(inputs, weights[0], preferred_element_type=jnp.float32)
-    up_out = jnp.dot(inputs, weights[1], preferred_element_type=jnp.float32)
-    return (jax.nn.silu(gate_out) * up_out).astype(jnp.bfloat16)
+PIECES = 2
+
+
+def pick_kernel(scale, chosen_ref, factor_ref, rows_ref, out_ref):
+    picked = jnp.dot(chosen_ref[0], rows_ref[0], preferred_element_type=jnp.float32)
+    if scale:
+        picked = factor_ref[0] * picked
+    out_ref[...] = picked.reshape(out_ref.shape).astype(out_ref.dtype)
+
+
+def pick(chosen, factor, rows, group, scale):
+    blocks, tok_count, width = rows.shape
+    picked_count = chosen.shape[1]
+    per_dest = picked_count // group
+    tile = min(width, 1024)
+    return pl.pallas_call(
+        functools.partial(pick_kernel, scale),
+        grid=(blocks, width // tile),
+        in_specs=[
+            pl.BlockSpec((1, picked_count, tok_count), lambda b, j: (b, 0, 0)),
+            pl.BlockSpec((1, picked_count, 1), lambda b, j: (b, 0, 0)),
+            pl.BlockSpec((1, tok_count, tile), lambda b, j: (b, 0, j)),
+        ],
+        out_specs=pl.BlockSpec((group, 1, per_dest, tile), lambda b, j: (0, b, 0, j)),
+        out_shape=jax.ShapeDtypeStruct((group, blocks, per_dest, width), rows.dtype),
+        compiler_params=pltpu.CompilerParams(vmem_limit_bytes=56 * 1024 * 1024),
+        cost_estimate=pl.CostEstimate(
+            flops=2 * blocks * picked_count * tok_count * width,
+            bytes_accessed=2 * blocks * (tok_count + picked_count) * width,
+            transcendentals=0,
+        ),
+    )(chosen, factor, rows)
 
 
 def body(
@@ -33,8 +65,15 @@
 
     routed = jnp.concatenate([routing.astype(jnp.float32), router_probs], axis=1)
     routed = lax.all_gather(routed, "dp", axis=0, tiled=False)
-    all_tokens = lax.all_gather(tokens, "dp", axis=0, tiled=False)
-    all_cotangent = lax.all_gather(cotangent, "dp", axis=0, tiled=False)
+    piece = model_width // PIECES
+    spans = [slice(p * piece, (p + 1) * piece) for p in range(PIECES)]
+    gathered = []
+    for source in (tokens, cotangent):
+        for span in spans:
+            part = source[:, span]
+            if gathered:
+                part, gathered[-1] = lax.optimization_barrier((part, gathered[-1]))
+            gathered.append(lax.all_gather(part, "dp", axis=0, tiled=False))
 
     first_expert = lax.axis_index("dp") * group
     own_experts = first_expert + jnp.arange(group, dtype=jnp.int32)
@@ -56,33 +95,40 @@
     chosen = column[:, :, None, :] == slots[None, None, :, None]
     factor = jnp.sum(jnp.where(chosen, weight[:, :, None, :], 0.0), axis=3)
     chosen = chosen.astype(jnp.bfloat16).reshape(dp_count, group * per_dest, tok_count)
-    factor = factor.reshape(dp_count, group * per_dest)
+    factor = factor.reshape(dp_count, group * per_dest, 1)
 
     def exchange(rows):
-        rows = rows.reshape(dp_count, group, per_dest, model_width).swapaxes(0, 1)
         rows = lax.all_to_all(rows, "expert", split_axis=0, concat_axis=0, tiled=True)
-        return rows.reshape(dp_count * group * per_dest, model_width)
+        return rows.reshape(dp_count * group * per_dest, piece)
 
-    token_rows = jnp.einsum(
-        "bst,btd->bsd", chosen, all_tokens, preferred_element_type=jnp.float32
-    ).astype(jnp.bfloat16)
-    inputs = exchange(token_rows)
-    cotangent_rows = jnp.einsum(
-        "bst,btd->bsd", chosen, all_cotangent, preferred_element_type=jnp.float32
+    arrived = []
+    for place, rows in enumerate(gathered):
+        arrived.append(exchange(pick(chosen, factor, rows, group, place >= PIECES)))
+    inputs, scaled = arrived[:PIECES], arrived[PIECES:]
+
+    gate_out = sum(
+        jnp.dot(x, gate_up[0, 0, span], preferred_element_type=jnp.float32)
+        for x, span in zip(inputs, spans)
     )
-    scaled = exchange((factor[:, :, None] * cotangent_rows).astype(jnp.bfloat16))
-
-    hidden = hidden_units(inputs, gate_up[0])
+    up_out = sum(
+        jnp.dot(x, gate_up[0, 1, span], preferred_element_type=jnp.float32)
+        for x, span in zip(inputs, spans)
+    )
+    hidden = (jax.nn.silu(gate_out) * up_out).astype(jnp.bfloat16)
     low = (
         adapter_scale_factor
         * jnp.einsum("pn,cn->pc", hidden, adapter_in[0], preferred_element_type=jnp.float32)
     ).astype(jnp.bfloat16)
-    back = (
-        adapter_scale_factor
-        * jnp.einsum("vw,cw->vc", scaled, adapter_out[0], preferred_element_type=jnp.float32)
-    ).astype(jnp.bfloat16)
+    back = sum(
+        jnp.einsum("vw,cw->vc", x, adapter_out[0, :, span], preferred_element_type=jnp.float32)
+        for x, span in zip(scaled, spans)
+    )
+    back = (adapter_scale_factor * back).astype(jnp.bfloat16)
     grad_first = jnp.einsum("mr,mf->rf", back, hidden, preferred_element_type=jnp.float32)
-    grad_second = jnp.einsum("mr,md->rd", low, scaled, preferred_element_type=jnp.float32)
+    grad_second = jnp.concatenate(
+        [jnp.einsum("mr,md->rd", low, x, preferred_element_type=jnp.float32) for x in scaled],
+        axis=1,
+    )
     return (grad_first[None], grad_second[None])
 
 

time: 330 us -> 314 us (0.952)
  waiting for transfers between devices: 222 us -> 184 us
  Pallas kernels: 0 us -> 29.9 us
  local copies, waits for them, and re-layouts: 15.6 us -> 4.83 us
  starting transfers between devices: 10.2 us -> 18.8 us
  matrix products: 49.7 us -> 42.5 us
    all_to_all x2 -> x4, waiting for transfers between devices: 71.7 us -> 22.2 us  [exchange(): lax.all_to_all(rows, 'expert', split_axis=0, concat_axis=0, tiled=True)]
    pallas_call x0 -> x4, Pallas kernels: none -> 29.9 us  [pick(): pl.pallas_call(functools.partial(pick_kernel, scale), grid=(blocks, width...]
    reshape x2 -> x1, local copies, waits for them, and re-layouts: 15.4 us -> 1.33 us  [body(): factor = factor.reshape(dp_count, group * per_dest, 1)]
    all_gather x2 -> x4, waiting for transfers between devices: 149 us -> 160 us  [body(): gathered.append(lax.all_gather(part, 'dp', axis=0, tiled=False))]
    all_to_all x2 -> x4, starting transfers between devices: 10.1 us -> 18.6 us  [exchange(): lax.all_to_all(rows, 'expert', split_axis=0, concat_axis=0, tiled=True)]
    dot_general x5 -> x8, matrix products: 42.7 us -> 37.9 us  [the longest x2 14.4 us: body(): jnp.dot(x, gate_up[0, 1, span], preferred_element_type=jnp.float32)]
    slice x0 -> x2, local copies, waits for them, and re-layouts: none -> 3.38 us  [body(): part = source[:, span]]
  transfers between devices with their start and end apart: 4 -> 8, of which waited for: 3 -> 5; matrix products, arithmetic and copies ran while one was open for 12% -> 13% of each run, Pallas kernels for 0% -> 7%
where the time goes in v2:
time: 314 us; the launch traced here: 313 us
  waiting for transfers between devices  184 us (59%)
  matrix products  42.5 us (14%)
  Pallas kernels  29.9 us (10%)
  starting transfers between devices  18.8 us (6%)
  blocking collectives  14.9 us (5%)
  between operations  13.9 us (4%)
  local copies, waits for them, and re-layouts  4.83 us (2%)
  other arithmetic  4.23 us (1%)
    all_gather x4, waiting for transfers between devices, body(): gathered.append(lax.all_gather(part, 'dp', axis=0, tiled=False))  160 us
    pallas_call x4, Pallas kernels, pick(): pl.pallas_call(functools.partial(pick_kernel, scale), grid=(blocks, width...  29.9 us
    all_to_all x4, waiting for transfers between devices, exchange(): lax.all_to_all(rows, 'expert', split_axis=0, concat_axis=0, tiled=True)  22.2 us
    all_to_all x4, starting transfers between devices, exchange(): lax.all_to_all(rows, 'expert', split_axis=0, concat_axis=0, tiled=True)  18.6 us
    all_gather x1, blocking collectives, body(): routed = lax.all_gather(routed, 'dp', axis=0, tiled=False)  14.9 us
    dot_general x2, matrix products, body(): jnp.dot(x, gate_up[0, 1, span], preferred_element_type=jnp.float32)  14.4 us
    dot_general x2, matrix products, body(): jnp.dot(x, gate_up[0, 0, span], preferred_element_type=jnp.float32)  13.4 us
  transfers between devices with their start and end apart: 8, of which 5 were waited for; matrix products, arithmetic and copies ran while one was open for 13% of the time, Pallas kernels for 7%

profile of v2, /device:TPU:0, one launch (start us, length us, event | category | flops | bytes accessed | tf_op | source)
XLA Modules:
  0.0 313.0 jit_solution(13445619051535982635)
XLA Ops:
  7.2 2.3 fusion.35
  9.6 0.7 convert_element_type.31
  10.3 0.7 pad_maximum_fusion
  11.0 14.9 %all-gather = f32[512,8]{0,1:T(8,128)S(1)} all-gather(f32[128,8]{0,1:T(8,128)S(1)} %pad_maximum_fusion), channel_id=2, replica_groups=mesh['dp'=4,'expert'=8] {'dp'}, dimensions={0}, use_global_device_ids=true | all-gather | bytes 20480 | tf_op jit(solution)/shard_map/all_gather | solution.py:67
  25.8 0.7 multiply_add_fusion
  27.1 1.3 reshape.43.factor_ref
  28.5 0.8 fusion.17.chosen_ref
  29.4 29.0 %all-gather.10.cloned.1.call-done = bf16[512,2048]{1,0:T(8,128)(2,1)} async-done(((bf16[128,2048]{1,0:T(8,128)(2,1)}), bf16[512,2048]{1,0:T(8,128)(2,1)}) %all-gather.10.cloned.1.call-update) | async-done | bytes 2097168 | tf_op jit(solution)/shard_map/all_gather | solution.py:76
  58.4 7.5 %shard_map.106 = bf16[8,4,32,2048]{3,2,1,0:T(8,128)(2,1)} custom-call(bf16[4,256,128]{2,1,0:T(8,128)(2,1)} %fusion.17.chosen_ref, f32[4,256,1]{2,1,0:T(8,128)} %reshape.43.factor_ref, bf16[4,128,2048]{2,1,0:T(8,128)(2,1)} %bitcast.59), custom_call_target="tpu_custom_call" | custom-call | flops 536870912 | bytes 6291456 | tf_op jit(solution)/shard_map/pallas_call | solution.py:28
  65.9 4.7 %all-to-all-start.2 = ((bf16[8,4,32,2048]{3,2,1,0:T(8,128)(2,1)}), bf16[8,4,32,2048]{3,2,1,0:T(8,128)(2,1)}, u32[]{:S(2)}, u32[]{:S(2)}) async-start(bf16[8,4,32,2048]{3,2,1,0:T(8,128)(2,1)} %shard_map.106), calls=%async_computation.2 | async-start | bytes 8388608 | tf_op jit(solution)/shard_map/all_to_all | solution.py:101
  70.6 0.7 all-gather.12.cloned.1.call-update
  71.4 1.1 fusion.34
  72.4 45.7 %all-gather.12.cloned.1.call-done = bf16[512,2048]{1,0:T(8,128)(2,1)} async-done(((bf16[128,2048]{1,0:T(8,128)(2,1)}), bf16[512,2048]{1,0:T(8,128)(2,1)}) %all-gather.12.cloned.1.call-update) | async-done | bytes 2097168 | tf_op jit(solution)/shard_map/all_gather | solution.py:76
  118.1 7.5 %shard_map.107 = bf16[8,4,32,2048]{3,2,1,0:T(8,128)(2,1)} custom-call(bf16[4,256,128]{2,1,0:T(8,128)(2,1)} %fusion.17.chosen_ref, f32[4,256,1]{2,1,0:T(8,128)} %reshape.43.factor_ref, bf16[4,128,2048]{2,1,0:T(8,128)(2,1)} %bitcast.60), custom_call_target="tpu_custom_call" | custom-call | flops 536870912 | bytes 6291456 | tf_op jit(solution)/shard_map/pallas_call | solution.py:28
  125.6 4.6 %all-to-all-start.3 = ((bf16[8,4,32,2048]{3,2,1,0:T(8,128)(2,1)}), bf16[8,4,32,2048]{3,2,1,0:T(8,128)(2,1)}, u32[]{:S(2)}, u32[]{:S(2)}) async-start(bf16[8,4,32,2048]{3,2,1,0:T(8,128)(2,1)} %shard_map.107), calls=%async_computation.3 | async-start | bytes 8388608 | tf_op jit(solution)/shard_map/all_to_all | solution.py:101
  130.2 0.7 all-gather.14.cloned.1.call-update
  130.9 46.8 %all-gather.14.cloned.1.call-done = bf16[512,2048]{1,0:T(8,128)(2,1)} async-done(((bf16[128,2048]{1,0:T(8,128)(2,1)}), bf16[512,2048]{1,0:T(8,128)(2,1)}) %all-gather.14.cloned.1.call-update) | async-done | bytes 2097168 | tf_op jit(solution)/shard_map/all_gather | solution.py:76
  177.7 7.5 %shard_map.104 = bf16[8,4,32,2048]{3,2,1,0:T(8,128)(2,1)} custom-call(bf16[4,256,128]{2,1,0:T(8,128)(2,1)} %fusion.17.chosen_ref, f32[4,256,1]{2,1,0:T(8,128)} %reshape.43.factor_ref, bf16[4,128,2048]{2,1,0:T(8,128)(2,1)} %bitcast.61), custom_call_target="tpu_custom_call" | custom-call | flops 536870912 | bytes 6291456 | tf_op jit(solution)/shard_map/pallas_call | solution.py:28
  185.1 4.6 %all-to-all-start = ((bf16[8,4,32,2048]{3,2,1,0:T(8,128)(2,1)}), bf16[8,4,32,2048]{3,2,1,0:T(8,128)(2,1)}, u32[]{:S(2)}, u32[]{:S(2)}) async-start(bf16[8,4,32,2048]{3,2,1,0:T(8,128)(2,1)} %shard_map.104), calls=%async_computation | async-start | bytes 8388608 | tf_op jit(solution)/shard_map/all_to_all | solution.py:101
  190.3 8.3 %fusion.2 = f32[1024,768]{1,0:T(8,128)} fusion(bf16[1024,2048]{1,0:T(8,128)(2,1)} %bitcast.11, bf16[1,2,4096,768]{3,2,1,0:T(8,128)(2,1)} %param.15), kind=kOutput, calls=%fused_computation.2 | convolution fusion | flops 3221225472 | bytes 10485760 | tf_op jit(solution)/shard_map/dot_general | solution.py:114
  198.6 38.4 %all-gather.16.cloned.1.call-done = bf16[512,2048]{1,0:T(8,128)(2,1)} async-done(((bf16[128,2048]{1,0:T(8,128)(2,1)}), bf16[512,2048]{1,0:T(8,128)(2,1)}) %all-gather.16.cloned.1.call-update) | async-done | bytes 2097168 | tf_op jit(solution)/shard_map/all_gather | solution.py:76
  237.0 7.5 %shard_map.105 = bf16[8,4,32,2048]{3,2,1,0:T(8,128)(2,1)} custom-call(bf16[4,256,128]{2,1,0:T(8,128)(2,1)} %fusion.17.chosen_ref, f32[4,256,1]{2,1,0:T(8,128)} %reshape.43.factor_ref, bf16[4,128,2048]{2,1,0:T(8,128)(2,1)} %bitcast.62), custom_call_target="tpu_custom_call" | custom-call | flops 536870912 | bytes 6291456 | tf_op jit(solution)/shard_map/pallas_call | solution.py:28
  244.4 4.8 %all-to-all-start.1 = ((bf16[8,4,32,2048]{3,2,1,0:T(8,128)(2,1)}), bf16[8,4,32,2048]{3,2,1,0:T(8,128)(2,1)}, u32[]{:S(2)}, u32[]{:S(2)}) async-start(bf16[8,4,32,2048]{3,2,1,0:T(8,128)(2,1)} %shard_map.105), calls=%async_computation.1 | async-start | bytes 8388608 | tf_op jit(solution)/shard_map/all_to_all | solution.py:101
  249.2 6.1 %fusion = f32[1024,768]{1,0:T(8,128)S(1)} fusion(bf16[1024,2048]{1,0:T(8,128)(2,1)} %bitcast.13, bf16[1,2,4096,768]{3,2,1,0:T(8,128)(2,1)} %param.15), kind=kOutput, calls=%fused_computation | convolution fusion | flops 3221225472 | bytes 10485760 | tf_op jit(solution)/shard_map/dot_general | solution.py:114
  255.4 6.3 %fusion.4 = f32[1024,768]{1,0:T(8,128)S(1)} fusion(bf16[1024,2048]{1,0:T(8,128)(2,1)} %bitcast.13, bf16[1,2,4096,768]{3,2,1,0:T(8,128)(2,1)} %param.15), kind=kOutput, calls=%fused_computation.4 | convolution fusion | flops 3221225472 | bytes 10485760 | tf_op jit(solution)/shard_map/dot_general | solution.py:110
  261.7 7.1 %multiply_convert_fusion = bf16[1024,768]{1,0:T(8,128)(2,1)S(1)} fusion(f32[1024,768]{1,0:T(8,128)S(1)} %copy-done.3, f32[1024,768]{1,0:T(8,128)S(1)} %fusion, f32[1024,768]{1,0:T(8,128)S(1)} %fusion.4, bf16[1024,2048]{1,0:T(8,128)(2,1)} %bitcast.11, bf16[1,2,4096,768]{3,2,1,0:T(8,128)(2,1)} %param.15), kind=kOutput, calls=%fused_computation.8 | convolution fusion | flops 3227516928 | bytes 18350080 | tf_op jit(solution)/shard_map/dot_general | solution.py:110
  269.4 3.5 %fusion.20 = f32[1024,32]{0,1:T(8,128)S(1)} fusion(bf16[1024,2048]{1,0:T(8,128)(2,1)} %bitcast.6, bf16[1,32,4096]{2,1,0:T(8,128)(2,1)S(1)} %copy-done.2), kind=kOutput, calls=%fused_computation.25 | convolution fusion | flops 134217728 | bytes 4456448 | tf_op jit(solution)/shard_map/vw,cw->vc/dot_general | solution.py:123
  272.9 3.0 fusion.37
  276.0 22.2 %all-to-all-done.1 = bf16[8,4,32,2048]{3,2,1,0:T(8,128)(2,1)} async-done(((bf16[8,4,32,2048]{3,2,1,0:T(8,128)(2,1)}), bf16[8,4,32,2048]{3,2,1,0:T(8,128)(2,1)}, u32[]{:S(2)}, u32[]{:S(2)}) %all-to-all-start.1) | async-done | bytes 4194336 | tf_op jit(solution)/shard_map/all_to_all | solution.py:101
  298.1 3.0 fusion.38
  301.2 4.5 %convolution_bitcast_fusion = f32[1,32,768]{2,1,0:T(8,128)} fusion(bf16[1024,768]{1,0:T(8,128)(2,1)S(1)} %multiply_convert_fusion, f32[1024,32]{0,1:T(8,128)S(1)} %fusion.20, bf16[1024,2048]{1,0:T(8,128)(2,1)} %bitcast.9, bf16[1,32,4096]{2,1,0:T(8,128)(2,1)S(1)} %copy-done.2), kind=kOutput, calls=%fused_computation.16 | convolution fusion | flops 184647680 | bytes 6127616 | tf_op jit(solution)/shard_map/mr,mf->rf/dot_general | solution.py:127
  305.7 0.8 maximum_bitcast_fusion
  (27 shorter events, 2.0 us)
Async XLA Ops:
  7.2 261.7 %copy-start = (bf16[1,32,768]{2,1,0:T(8,128)(2,1)S(1)}, bf16[1,32,768]{2,1,0:T(8,128)(2,1)}, u32[]{:S(2)}) copy-start(bf16[1,32,768]{2,1,0:T(8,128)(2,1)} %param.16) | copy-start | bytes 147460
  7.2 51.2 %all-gather.10.cloned.1.call-start = ((), (), s32[]{:S(2)}) async-start(), calls=%async_computation.4 | async-start | bytes 2621440 | tf_op jit(solution)/shard_map/all_gather | solution.py:76
  65.9 5.5 %copy-start.1 = (bf16[128,4096]{1,0:T(8,128)(2,1)S(1)}, bf16[128,4096]{1,0:T(8,128)(2,1)}, u32[]{:S(2)}) copy-start(bf16[128,4096]{1,0:T(8,128)(2,1)} %param.10) | copy-start | bytes 3145732
  65.9 59.7 %all-to-all-start.2 = ((bf16[8,4,32,2048]{3,2,1,0:T(8,128)(2,1)}), bf16[8,4,32,2048]{3,2,1,0:T(8,128)(2,1)}, u32[]{:S(2)}, u32[]{:S(2)}) async-start(bf16[8,4,32,2048]{3,2,1,0:T(8,128)(2,1)} %shard_map.106), calls=%async_computation.2 | async-start | bytes 8388608 | tf_op jit(solution)/shard_map/all_to_all | solution.py:101
  70.6 47.5 %all-gather.12.cloned.1.call-start = ((), (), s32[]{:S(2)}) async-start(), calls=%async_computation.5 | async-start | bytes 2621440 | tf_op jit(solution)/shard_map/all_gather | solution.py:76
  125.6 59.5 %all-to-all-start.3 = ((bf16[8,4,32,2048]{3,2,1,0:T(8,128)(2,1)}), bf16[8,4,32,2048]{3,2,1,0:T(8,128)(2,1)}, u32[]{:S(2)}, u32[]{:S(2)}) async-start(bf16[8,4,32,2048]{3,2,1,0:T(8,128)(2,1)} %shard_map.107), calls=%async_computation.3 | async-start | bytes 8388608 | tf_op jit(solution)/shard_map/all_to_all | solution.py:101
  130.2 47.5 %all-gather.14.cloned.1.call-start = ((), (), s32[]{:S(2)}) async-start(), calls=%async_computation.6 | async-start | bytes 2621440 | tf_op jit(solution)/shard_map/all_gather | solution.py:76
  185.1 59.3 %all-to-all-start = ((bf16[8,4,32,2048]{3,2,1,0:T(8,128)(2,1)}), bf16[8,4,32,2048]{3,2,1,0:T(8,128)(2,1)}, u32[]{:S(2)}, u32[]{:S(2)}) async-start(bf16[8,4,32,2048]{3,2,1,0:T(8,128)(2,1)} %shard_map.104), calls=%async_computation | async-start | bytes 8388608 | tf_op jit(solution)/shard_map/all_to_all | solution.py:101
  189.7 47.2 %all-gather.16.cloned.1.call-start = ((), (), s32[]{:S(2)}) async-start(), calls=%async_computation.7 | async-start | bytes 2621440 | tf_op jit(solution)/shard_map/all_gather | solution.py:76
  244.4 53.7 %all-to-all-start.1 = ((bf16[8,4,32,2048]{3,2,1,0:T(8,128)(2,1)}), bf16[8,4,32,2048]{3,2,1,0:T(8,128)(2,1)}, u32[]{:S(2)}, u32[]{:S(2)}) async-start(bf16[8,4,32,2048]{3,2,1,0:T(8,128)(2,1)} %shard_map.105), calls=%async_computation.1 | async-start | bytes 8388608 | tf_op jit(solution)/shard_map/all_to_all | solution.py:101
  255.3 6.3 %copy-start.3 = (f32[1024,768]{1,0:T(8,128)S(1)}, f32[1024,768]{1,0:T(8,128)}, u32[]{:S(2)}) copy-start(f32[1024,768]{1,0:T(8,128)} %fusion.2) | copy-start | bytes 9437188
  261.7 7.7 %copy-start.2 = (bf16[1,32,4096]{2,1,0:T(8,128)(2,1)S(1)}, bf16[1,32,4096]{2,1,0:T(8,128)(2,1)}, u32[]{:S(2)}) copy-start(bf16[1,32,4096]{2,1,0:T(8,128)(2,1)} %param.17) | copy-start | bytes 786436
Sparse Core Ops, SparseCore 0:
  9.7 48.6 all-gather.9
  73.0 45.0 all-gather.11
  132.6 45.0 all-gather.13
  191.8 45.0 all-gather.15

commit v3 on v2

--- a/solution.py
+++ b/solution.py
@@ -37,8 +37,8 @@
         out_shape=jax.ShapeDtypeStruct((group, blocks, per_dest, width), rows.dtype),
         compiler_params=pltpu.CompilerParams(vmem_limit_bytes=56 * 1024 * 1024),
         cost_estimate=pl.CostEstimate(
-            flops=2 * blocks * picked_count * tok_count * width,
-            bytes_accessed=2 * blocks * (tok_count + picked_count) * width,
+            flops=64 * blocks * picked_count * tok_count * width,
+            bytes_accessed=64 * blocks * (tok_count + picked_count) * width,
             transcendentals=0,
         ),
     )(chosen, factor, rows)

time: 314 us -> 297 us (0.946)
  waiting for transfers between devices: 184 us -> 167 us
    all_gather x4, waiting for transfers between devices: 160 us -> 99.8 us  [body(): gathered.append(lax.all_gather(part, 'dp', axis=0, tiled=False))]
    all_to_all x4, waiting for transfers between devices: 22.2 us -> 66.8 us  [exchange(): lax.all_to_all(rows, 'expert', split_axis=0, concat_axis=0, tiled=True)]
  transfers between devices with their start and end apart: 8 -> 8, of which waited for: 5 -> 8; matrix products, arithmetic and copies ran while one was open for 13% -> 14% of each run, Pallas kernels for 7% -> 10%
where the time goes in v3:
time: 297 us; the launch traced here: 296 us
  waiting for transfers between devices  167 us (56%)
  matrix products  42.6 us (14%)
  Pallas kernels  29.9 us (10%)
  starting transfers between devices  18.8 us (6%)
  blocking collectives  14.8 us (5%)
  between operations  13.9 us (5%)
  local copies, waits for them, and re-layouts  4.83 us (2%)
  other arithmetic  4.23 us (1%)
    all_gather x4, waiting for transfers between devices, body(): gathered.append(lax.all_gather(part, 'dp', axis=0, tiled=False))  99.8 us
    all_to_all x4, waiting for transfers between devices, exchange(): lax.all_to_all(rows, 'expert', split_axis=0, concat_axis=0, tiled=True)  66.8 us
    pallas_call x4, Pallas kernels, pick(): pl.pallas_call(functools.partial(pick_kernel, scale), grid=(blocks, width...  29.9 us
    all_to_all x4, starting transfers between devices, exchange(): lax.all_to_all(rows, 'expert', split_axis=0, concat_axis=0, tiled=True)  18.6 us
    all_gather x1, blocking collectives, body(): routed = lax.all_gather(routed, 'dp', axis=0, tiled=False)  14.8 us
    dot_general x2, matrix products, body(): jnp.dot(x, gate_up[0, 1, span], preferred_element_type=jnp.float32)  14.4 us
    dot_general x2, matrix products, body(): jnp.dot(x, gate_up[0, 0, span], preferred_element_type=jnp.float32)  13.4 us
    dot_general x2, matrix products, body(): jnp.einsum('mr,md->rd', low, x, preferred_element_type=jnp.float32)  6.03 us
  transfers between devices with their start and end apart: 8, of which 8 were waited for; matrix products, arithmetic and copies ran while one was open for 14% of the time, Pallas kernels for 10%

profile of v3, /device:TPU:0, one launch (start us, length us, event | category | flops | bytes accessed | tf_op | source)
XLA Modules:
  0.0 295.8 jit_solution(16724078029545469307)
XLA Ops:
  7.2 2.3 fusion.35
  9.6 0.7 convert_element_type.31
  10.3 0.7 pad_maximum_fusion
  11.0 14.8 %all-gather = f32[512,8]{0,1:T(8,128)S(1)} all-gather(f32[128,8]{0,1:T(8,128)S(1)} %pad_maximum_fusion), channel_id=2, replica_groups=mesh['dp'=4,'expert'=8] {'dp'}, dimensions={0}, use_global_device_ids=true | all-gather | bytes 20480 | tf_op jit(solution)/shard_map/all_gather | solution.py:67
  27.2 1.3 reshape.43.factor_ref
  28.6 0.8 fusion.17.chosen_ref
  29.4 29.0 %all-gather.10.cloned.1.call-done = bf16[512,2048]{1,0:T(8,128)(2,1)} async-done(((bf16[128,2048]{1,0:T(8,128)(2,1)}), bf16[512,2048]{1,0:T(8,128)(2,1)}) %all-gather.10.cloned.1.call-update) | async-done | bytes 2097168 | tf_op jit(solution)/shard_map/all_gather | solution.py:76
  58.4 7.5 %shard_map.106 = bf16[8,4,32,2048]{3,2,1,0:T(8,128)(2,1)} custom-call(bf16[4,256,128]{2,1,0:T(8,128)(2,1)} %fusion.17.chosen_ref, f32[4,256,1]{2,1,0:T(8,128)} %reshape.43.factor_ref, bf16[4,128,2048]{2,1,0:T(8,128)(2,1)} %bitcast.60), custom_call_target="tpu_custom_call" | custom-call | flops 17179869184 | bytes 201326592 | tf_op jit(solution)/shard_map/pallas_call | solution.py:28
  65.9 4.7 %all-to-all-start.2 = ((bf16[8,4,32,2048]{3,2,1,0:T(8,128)(2,1)}), bf16[8,4,32,2048]{3,2,1,0:T(8,128)(2,1)}, u32[]{:S(2)}, u32[]{:S(2)}) async-start(bf16[8,4,32,2048]{3,2,1,0:T(8,128)(2,1)} %shard_map.106), calls=%async_computation.2 | async-start | bytes 8388608 | tf_op jit(solution)/shard_map/all_to_all | solution.py:101
  70.7 1.1 fusion.34
  71.8 32.9 %all-gather.12.cloned.1.call-done = bf16[512,2048]{1,0:T(8,128)(2,1)} async-done(((bf16[128,2048]{1,0:T(8,128)(2,1)}), bf16[512,2048]{1,0:T(8,128)(2,1)}) %all-gather.12.cloned.1.call-update) | async-done | bytes 2097168 | tf_op jit(solution)/shard_map/all_gather | solution.py:76
  104.7 7.5 %shard_map.107 = bf16[8,4,32,2048]{3,2,1,0:T(8,128)(2,1)} custom-call(bf16[4,256,128]{2,1,0:T(8,128)(2,1)} %fusion.17.chosen_ref, f32[4,256,1]{2,1,0:T(8,128)} %reshape.43.factor_ref, bf16[4,128,2048]{2,1,0:T(8,128)(2,1)} %bitcast.62), custom_call_target="tpu_custom_call" | custom-call | flops 17179869184 | bytes 201326592 | tf_op jit(solution)/shard_map/pallas_call | solution.py:28
  112.1 7.6 %all-to-all-done.2 = bf16[8,4,32,2048]{3,2,1,0:T(8,128)(2,1)} async-done(((bf16[8,4,32,2048]{3,2,1,0:T(8,128)(2,1)}), bf16[8,4,32,2048]{3,2,1,0:T(8,128)(2,1)}, u32[]{:S(2)}, u32[]{:S(2)}) %all-to-all-start.2) | async-done | bytes 4194336 | tf_op jit(solution)/shard_map/all_to_all | solution.py:101
  119.8 4.6 %all-to-all-start.3 = ((bf16[8,4,32,2048]{3,2,1,0:T(8,128)(2,1)}), bf16[8,4,32,2048]{3,2,1,0:T(8,128)(2,1)}, u32[]{:S(2)}, u32[]{:S(2)}) async-start(bf16[8,4,32,2048]{3,2,1,0:T(8,128)(2,1)} %shard_map.107), calls=%async_computation.3 | async-start | bytes 8388608 | tf_op jit(solution)/shard_map/all_to_all | solution.py:101
  124.4 26.9 %all-gather.14.cloned.1.call-done = bf16[512,2048]{1,0:T(8,128)(2,1)} async-done(((bf16[128,2048]{1,0:T(8,128)(2,1)}), bf16[512,2048]{1,0:T(8,128)(2,1)}) %all-gather.14.cloned.1.call-update) | async-done | bytes 2097168 | tf_op jit(solution)/shard_map/all_gather | solution.py:76
  151.3 7.5 %shard_map.104 = bf16[8,4,32,2048]{3,2,1,0:T(8,128)(2,1)} custom-call(bf16[4,256,128]{2,1,0:T(8,128)(2,1)} %fusion.17.chosen_ref, f32[4,256,1]{2,1,0:T(8,128)} %reshape.43.factor_ref, bf16[4,128,2048]{2,1,0:T(8,128)(2,1)} %bitcast.61), custom_call_target="tpu_custom_call" | custom-call | flops 17179869184 | bytes 201326592 | tf_op jit(solution)/shard_map/pallas_call | solution.py:28
  158.8 14.7 %all-to-all-done.3 = bf16[8,4,32,2048]{3,2,1,0:T(8,128)(2,1)} async-done(((bf16[8,4,32,2048]{3,2,1,0:T(8,128)(2,1)}), bf16[8,4,32,2048]{3,2,1,0:T(8,128)(2,1)}, u32[]{:S(2)}, u32[]{:S(2)}) %all-to-all-start.3) | async-done | bytes 4194336 | tf_op jit(solution)/shard_map/all_to_all | solution.py:101
  173.5 4.6 %all-to-all-start = ((bf16[8,4,32,2048]{3,2,1,0:T(8,128)(2,1)}), bf16[8,4,32,2048]{3,2,1,0:T(8,128)(2,1)}, u32[]{:S(2)}, u32[]{:S(2)}) async-start(bf16[8,4,32,2048]{3,2,1,0:T(8,128)(2,1)} %shard_map.104), calls=%async_computation | async-start | bytes 8388608 | tf_op jit(solution)/shard_map/all_to_all | solution.py:101
  178.1 8.3 %fusion.2 = f32[1024,768]{1,0:T(8,128)} fusion(bf16[1024,2048]{1,0:T(8,128)(2,1)} %bitcast.11, bf16[1,2,4096,768]{3,2,1,0:T(8,128)(2,1)} %param.15), kind=kOutput, calls=%fused_computation.2 | convolution fusion | flops 3221225472 | bytes 10485760 | tf_op jit(solution)/shard_map/dot_general | solution.py:114
  186.4 11.0 %all-gather.16.cloned.1.call-done = bf16[512,2048]{1,0:T(8,128)(2,1)} async-done(((bf16[128,2048]{1,0:T(8,128)(2,1)}), bf16[512,2048]{1,0:T(8,128)(2,1)}) %all-gather.16.cloned.1.call-update) | async-done | bytes 2097168 | tf_op jit(solution)/shard_map/all_gather | solution.py:76
  197.3 7.5 %shard_map.105 = bf16[8,4,32,2048]{3,2,1,0:T(8,128)(2,1)} custom-call(bf16[4,256,128]{2,1,0:T(8,128)(2,1)} %fusion.17.chosen_ref, f32[4,256,1]{2,1,0:T(8,128)} %reshape.43.factor_ref, bf16[4,128,2048]{2,1,0:T(8,128)(2,1)} %bitcast.63), custom_call_target="tpu_custom_call" | custom-call | flops 17179869184 | bytes 201326592 | tf_op jit(solution)/shard_map/pallas_call | solution.py:28
  204.8 22.4 %all-to-all-done = bf16[8,4,32,2048]{3,2,1,0:T(8,128)(2,1)} async-done(((bf16[8,4,32,2048]{3,2,1,0:T(8,128)(2,1)}), bf16[8,4,32,2048]{3,2,1,0:T(8,128)(2,1)}, u32[]{:S(2)}, u32[]{:S(2)}) %all-to-all-start) | async-done | bytes 4194336 | tf_op jit(solution)/shard_map/all_to_all | solution.py:101
  227.2 4.8 %all-to-all-start.1 = ((bf16[8,4,32,2048]{3,2,1,0:T(8,128)(2,1)}), bf16[8,4,32,2048]{3,2,1,0:T(8,128)(2,1)}, u32[]{:S(2)}, u32[]{:S(2)}) async-start(bf16[8,4,32,2048]{3,2,1,0:T(8,128)(2,1)} %shard_map.105), calls=%async_computation.1 | async-start | bytes 8388608 | tf_op jit(solution)/shard_map/all_to_all | solution.py:101
  232.0 6.1 %fusion = f32[1024,768]{1,0:T(8,128)S(1)} fusion(bf16[1024,2048]{1,0:T(8,128)(2,1)} %bitcast.13, bf16[1,2,4096,768]{3,2,1,0:T(8,128)(2,1)} %param.15), kind=kOutput, calls=%fused_computation | convolution fusion | flops 3221225472 | bytes 10485760 | tf_op jit(solution)/shard_map/dot_general | solution.py:114
  238.1 6.3 %fusion.4 = f32[1024,768]{1,0:T(8,128)S(1)} fusion(bf16[1024,2048]{1,0:T(8,128)(2,1)} %bitcast.13, bf16[1,2,4096,768]{3,2,1,0:T(8,128)(2,1)} %param.15), kind=kOutput, calls=%fused_computation.4 | convolution fusion | flops 3221225472 | bytes 10485760 | tf_op jit(solution)/shard_map/dot_general | solution.py:110
  244.4 7.1 %multiply_convert_fusion = bf16[1024,768]{1,0:T(8,128)(2,1)S(1)} fusion(f32[1024,768]{1,0:T(8,128)S(1)} %copy-done.3, f32[1024,768]{1,0:T(8,128)S(1)} %fusion, f32[1024,768]{1,0:T(8,128)S(1)} %fusion.4, bf16[1024,2048]{1,0:T(8,128)(2,1)} %bitcast.11, bf16[1,2,4096,768]{3,2,1,0:T(8,128)(2,1)} %param.15), kind=kOutput, calls=%fused_computation.8 | convolution fusion | flops 3227516928 | bytes 18350080 | tf_op jit(solution)/shard_map/dot_general | solution.py:110
  252.2 3.5 %fusion.20 = f32[1024,32]{0,1:T(8,128)S(1)} fusion(bf16[1024,2048]{1,0:T(8,128)(2,1)} %bitcast.6, bf16[1,32,4096]{2,1,0:T(8,128)(2,1)S(1)} %copy-done.2), kind=kOutput, calls=%fused_computation.25 | convolution fusion | flops 134217728 | bytes 4456448 | tf_op jit(solution)/shard_map/vw,cw->vc/dot_general | solution.py:123
  255.7 3.0 %fusion.37 = f32[32,2048]{1,0:T(8,128)S(1)} fusion(bf16[1024,32]{0,1:T(8,128)(2,1)S(1)} %fusion.15, bf16[1024,2048]{1,0:T(8,128)(2,1)} %bitcast.6), kind=kOutput, calls=%fused_computation.46 | convolution fusion | flops 134217728 | bytes 4521984 | tf_op jit(solution)/shard_map/mr,md->rd/dot_general | solution.py:129
  258.7 22.2 %all-to-all-done.1 = bf16[8,4,32,2048]{3,2,1,0:T(8,128)(2,1)} async-done(((bf16[8,4,32,2048]{3,2,1,0:T(8,128)(2,1)}), bf16[8,4,32,2048]{3,2,1,0:T(8,128)(2,1)}, u32[]{:S(2)}, u32[]{:S(2)}) %all-to-all-start.1) | async-done | bytes 4194336 | tf_op jit(solution)/shard_map/all_to_all | solution.py:101
  280.9 3.0 %fusion.38 = f32[32,2048]{1,0:T(8,128)S(1)} fusion(bf16[1024,32]{0,1:T(8,128)(2,1)S(1)} %fusion.15, bf16[1024,2048]{1,0:T(8,128)(2,1)} %bitcast.9), kind=kOutput, calls=%fused_computation.47 | convolution fusion | flops 134217728 | bytes 4521984 | tf_op jit(solution)/shard_map/mr,md->rd/dot_general | solution.py:129
  283.9 4.5 %convolution_bitcast_fusion = f32[1,32,768]{2,1,0:T(8,128)} fusion(bf16[1024,768]{1,0:T(8,128)(2,1)S(1)} %multiply_convert_fusion, f32[1024,32]{0,1:T(8,128)S(1)} %fusion.20, bf16[1024,2048]{1,0:T(8,128)(2,1)} %bitcast.9, bf16[1,32,4096]{2,1,0:T(8,128)(2,1)S(1)} %copy-done.2), kind=kOutput, calls=%fused_computation.16 | convolution fusion | flops 184647680 | bytes 6127616 | tf_op jit(solution)/shard_map/mr,mf->rf/dot_general | solution.py:127
  288.4 0.8 maximum_bitcast_fusion
  (27 shorter events, 2.2 us)
Async XLA Ops:
  7.2 244.4 %copy-start = (bf16[1,32,768]{2,1,0:T(8,128)(2,1)S(1)}, bf16[1,32,768]{2,1,0:T(8,128)(2,1)}, u32[]{:S(2)}) copy-start(bf16[1,32,768]{2,1,0:T(8,128)(2,1)} %param.16) | copy-start | bytes 147460
  7.2 51.2 %all-gather.10.cloned.1.call-start = ((), (), s32[]{:S(2)}) async-start(), calls=%async_computation.4 | async-start | bytes 2621440 | tf_op jit(solution)/shard_map/all_gather | solution.py:76
  9.6 95.1 %all-gather.12.cloned.1.call-start = ((), (), s32[]{:S(2)}) async-start(), calls=%async_computation.5 | async-start | bytes 2621440 | tf_op jit(solution)/shard_map/all_gather | solution.py:76
  65.9 4.8 %copy-start.1 = (bf16[128,4096]{1,0:T(8,128)(2,1)S(1)}, bf16[128,4096]{1,0:T(8,128)(2,1)}, u32[]{:S(2)}) copy-start(bf16[128,4096]{1,0:T(8,128)(2,1)} %param.10) | copy-start | bytes 3145732
  65.9 53.8 %all-to-all-start.2 = ((bf16[8,4,32,2048]{3,2,1,0:T(8,128)(2,1)}), bf16[8,4,32,2048]{3,2,1,0:T(8,128)(2,1)}, u32[]{:S(2)}, u32[]{:S(2)}) async-start(bf16[8,4,32,2048]{3,2,1,0:T(8,128)(2,1)} %shard_map.106), calls=%async_computation.2 | async-start | bytes 8388608 | tf_op jit(solution)/shard_map/all_to_all | solution.py:101
  70.6 80.7 %all-gather.14.cloned.1.call-start = ((), (), s32[]{:S(2)}) async-start(), calls=%async_computation.6 | async-start | bytes 2621440 | tf_op jit(solution)/shard_map/all_gather | solution.py:76
  119.8 53.7 %all-to-all-start.3 = ((bf16[8,4,32,2048]{3,2,1,0:T(8,128)(2,1)}), bf16[8,4,32,2048]{3,2,1,0:T(8,128)(2,1)}, u32[]{:S(2)}, u32[]{:S(2)}) async-start(bf16[8,4,32,2048]{3,2,1,0:T(8,128)(2,1)} %shard_map.107), calls=%async_computation.3 | async-start | bytes 8388608 | tf_op jit(solution)/shard_map/all_to_all | solution.py:101
  124.3 73.0 %all-gather.16.cloned.1.call-start = ((), (), s32[]{:S(2)}) async-start(), calls=%async_computation.7 | async-start | bytes 2621440 | tf_op jit(solution)/shard_map/all_gather | solution.py:76
  173.5 53.7 %all-to-all-start = ((bf16[8,4,32,2048]{3,2,1,0:T(8,128)(2,1)}), bf16[8,4,32,2048]{3,2,1,0:T(8,128)(2,1)}, u32[]{:S(2)}, u32[]{:S(2)}) async-start(bf16[8,4,32,2048]{3,2,1,0:T(8,128)(2,1)} %shard_map.104), calls=%async_computation | async-start | bytes 8388608 | tf_op jit(solution)/shard_map/all_to_all | solution.py:101
  227.2 53.7 %all-to-all-start.1 = ((bf16[8,4,32,2048]{3,2,1,0:T(8,128)(2,1)}), bf16[8,4,32,2048]{3,2,1,0:T(8,128)(2,1)}, u32[]{:S(2)}, u32[]{:S(2)}) async-start(bf16[8,4,32,2048]{3,2,1,0:T(8,128)(2,1)} %shard_map.105), calls=%async_computation.1 | async-start | bytes 8388608 | tf_op jit(solution)/shard_map/all_to_all | solution.py:101
  238.1 6.3 %copy-start.3 = (f32[1024,768]{1,0:T(8,128)S(1)}, f32[1024,768]{1,0:T(8,128)}, u32[]{:S(2)}) copy-start(f32[1024,768]{1,0:T(8,128)} %fusion.2) | copy-start | bytes 9437188
  244.4 7.7 %copy-start.2 = (bf16[1,32,4096]{2,1,0:T(8,128)(2,1)S(1)}, bf16[1,32,4096]{2,1,0:T(8,128)(2,1)}, u32[]{:S(2)}) copy-start(bf16[1,32,4096]{2,1,0:T(8,128)(2,1)} %param.17) | copy-start | bytes 786436
Sparse Core Ops, SparseCore 0:
  9.7 48.6 all-gather.9
  60.0 44.6 all-gather.11
  106.2 45.0 all-gather.13
  152.7 44.5 all-gather.15
